TPU v7x, 32 devices: a whole 2x2x4 slice. The times are simulated.
32 devices in a mesh: ha: 4 (over z), wa: 8 (over y, x, core).
Axes of the slice: x: 2, y: 2, z: 4, core: 2. Of those that a mesh axis runs over, the one named last changes fastest.
Arguments:
- features: bfloat16 [128, 256, 256], P('ha', 'wa'), may hold values from -6 to 6
- counts: int32 [4, 8], P('ha', 'wa'), may hold values from 0 to 16, as said below
- owner_perm: int32 [4, 8], P('ha'), may hold values from 0 to 7, each once within a row
- corners: int32 [512, 2], P(('ha', 'wa')), may hold values from 0 to 31, as said below
- offsets: int32 [512, 28], P(('ha', 'wa')), may hold values from 0 to 124
- kernels: bfloat16 [2, 3, 3, 256, 256], replicated, may hold values from -0.125 to 0.125
- cotangent: bfloat16 [256, 14, 14, 256], P(('ha', 'wa')), may hold values from -6 to 6
Outputs:
- grad_features: float32 [128, 256, 256], P('ha', 'wa')
- grad_kernels: float32 [2, 3, 3, 256, 256], replicated
Inputs may be any that keep to these rules, and one draw needn't show every extreme that they name: In each row of tiles the counts add up to 8 times the number of devices along wa, and one tile of every row has exactly 16. `corners`: the first column is below 32, the second below 32.
All inputs are finite; a program needn't handle non-finite values.
Results may differ from a plain program's by a relative error of at most 0.012.
Values may be sent and summed in bfloat16 or wider, within the bound.
A program may use at most 192 MiB of HBM per device.

v0:
```python
import jax
import jax.numpy as jnp
from jax import lax
from jax.sharding import PartitionSpec as P

SIDE = 14
BOX = 32
LAYERS = 2


highest = lax.Precision.HIGHEST


def shifted(value, axis, steps):
    count = lax.axis_size(axis)
    first, last = (max(0, -steps), min(count, count - steps))
    return lax.ppermute(value, axis, [(source, source + steps) for source in range(first, last)])


def placed_weights(sample_offsets, corner_at, span):
    places = 4 * (jnp.arange(span, dtype=jnp.int32)[None, :] - corner_at[:, None])
    spread = jnp.abs(places[:, None, :] - sample_offsets[:, :, None]).astype(jnp.float32)
    return jnp.maximum(0.0, 1.0 - spread / 4.0)


def gelu_exact(values):
    return jax.nn.gelu(values, approximate=False)


def patches_of(inputs):
    amount, channels = (inputs.shape[0], inputs.shape[3])
    padded = jnp.pad(inputs, ((0, 0), (1, 1), (1, 1), (0, 0)))
    pieces = []
    for row_step in range(3):
        for col_step in range(3):
            pieces.append(padded[:, row_step : row_step + SIDE, col_step : col_step + SIDE, :])
    return jnp.concatenate(pieces, axis=3).reshape(amount * SIDE * SIDE, 9 * channels)


def fold_back(columns, amount):
    channels = columns.shape[1] // 9
    pieces = columns.reshape(amount, SIDE, SIDE, 9, channels)
    totals = jnp.zeros((amount, SIDE + 2, SIDE + 2, channels), jnp.float32)
    for row_step in range(3):
        for col_step in range(3):
            totals = totals.at[:, row_step : row_step + SIDE, col_step : col_step + SIDE, :].add(
                pieces[:, :, :, 3 * row_step + col_step, :]
            )
    return totals[:, 1 : SIDE + 1, 1 : SIDE + 1, :]


def mask_head(samples, upstream, kernels):
    amount, channels = (samples.shape[0], samples.shape[3])
    inputs = samples
    saved = []
    for layer_step in range(LAYERS):
        matrix = kernels[layer_step].reshape(9 * channels, channels)
        columns = patches_of(inputs)
        before = jnp.dot(columns, matrix, preferred_element_type=jnp.float32)
        saved.append((columns, before, matrix))
        if layer_step + 1 < LAYERS:
            inputs = gelu_exact(before).astype(jnp.bfloat16).reshape(amount, SIDE, SIDE, channels)
    upward = upstream.reshape(amount * SIDE * SIDE, channels)
    kernel_grads = [None] * LAYERS
    for layer_step in reversed(range(LAYERS)):
        columns, before, matrix = saved[layer_step]
        ignored, gelu_slope = jax.vjp(gelu_exact, before)
        inner_grad = gelu_slope(upward.astype(jnp.float32))[0].astype(jnp.bfloat16)
        layer_grad = lax.dot_general(
            columns, inner_grad, (((0,), (0,)), ((), ())), preferred_element_type=jnp.float32
        )
        kernel_grads[layer_step] = layer_grad
        spread = lax.dot_general(
            inner_grad, matrix, (((1,), (1,)), ((), ())), preferred_element_type=jnp.float32
        )
        upward = (
            fold_back(spread, amount).astype(jnp.bfloat16).reshape(amount * SIDE * SIDE, channels)
        )
    return (upward.reshape(amount, SIDE * SIDE * channels), jnp.stack(kernel_grads))


def local(features, counts, owner_perm, corners, offsets, kernels, cotangent):
    tile_rows, tile_cols, channels = features.shape
    slot_total = corners.shape[0]
    owned = cotangent.shape[0]
    width_count = lax.axis_size("wa")
    pairs = slot_total // width_count
    col_index = lax.axis_index("wa")
    right_edge = shifted(features, "wa", -1)
    widened = jnp.concatenate([features, right_edge], axis=1)
    lower_edge = shifted(widened, "ha", -1)
    extended = jnp.concatenate([widened, lower_edge], axis=0)
    row_place = placed_weights(offsets[:, :SIDE], corners[:, 0], tile_rows + BOX)
    col_place = placed_weights(offsets[:, SIDE:], corners[:, 1], tile_cols + BOX)
    partial_rows = jnp.einsum(
        "siy,yxc->sixc",
        row_place.astype(jnp.bfloat16),
        extended,
        preferred_element_type=jnp.float32,
    )
    samples = jnp.einsum("sjx,sixc->sijc", col_place, partial_rows, precision=highest).astype(
        jnp.bfloat16
    )
    row_counts = lax.all_gather(counts, "wa", axis=1, tiled=True)[0]
    starts = jnp.cumsum(row_counts) - row_counts
    device_ids = jnp.arange(width_count, dtype=jnp.int32)
    here_start = jnp.sum(jnp.where(device_ids == col_index, starts, 0))
    perm_row = owner_perm[0]
    slot_ids = jnp.arange(slot_total, dtype=jnp.int32)
    stream = here_start + slot_ids
    owner_of = jnp.sum(
        jnp.where((stream % width_count)[:, None] == device_ids[None, :], perm_row[None, :], 0),
        axis=1,
    )
    buffer_ids = jnp.arange(width_count * pairs, dtype=jnp.int32)
    live_slot = slot_ids < counts[0, 0]
    home_route = (
        ((owner_of * pairs + slot_ids // width_count)[:, None] == buffer_ids[None, :])
        & live_slot[:, None]
    ).astype(jnp.bfloat16)
    position = jnp.sum(jnp.where(perm_row == col_index, device_ids, 0))
    sender_match = (buffer_ids // pairs)[:, None] == device_ids[None, :]
    sender_start = jnp.sum(jnp.where(sender_match, starts[None, :], 0), axis=1)
    sender_count = jnp.sum(jnp.where(sender_match, row_counts[None, :], 0), axis=1)
    arrival = (
        sender_start + (position - sender_start) % width_count + buffer_ids % pairs * width_count
    )
    arrived = arrival < sender_start + sender_count
    own_route = (
        ((arrival // width_count)[None, :] == jnp.arange(owned, dtype=jnp.int32)[:, None])
        & arrived[None, :]
    ).astype(jnp.bfloat16)
    outgoing = jnp.dot(
        own_route.T,
        cotangent.reshape(owned, SIDE * SIDE * channels),
        preferred_element_type=jnp.float32,
    ).astype(jnp.bfloat16)
    incoming = lax.all_to_all(outgoing, "wa", split_axis=0, concat_axis=0, tiled=True)
    upstream = jnp.dot(home_route, incoming, preferred_element_type=jnp.float32).astype(
        jnp.bfloat16
    )
    home_grads, kernel_grads = mask_head(samples, upstream, kernels)
    kernel_grads = lax.psum(kernel_grads, ("ha", "wa"))
    sample_grads = home_grads.reshape(slot_total, SIDE, SIDE, channels)
    spread_cols = jnp.einsum(
        "sjx,sijc->sixc", col_place, sample_grads.astype(jnp.float32), precision=highest
    )
    grads_ext = jnp.einsum("siy,sixc->yxc", row_place, spread_cols, precision=highest)
    from_above = shifted(grads_ext[tile_rows:], "ha", 1)
    grads_ext = grads_ext.at[:BOX].add(from_above)
    from_left = shifted(grads_ext[:tile_rows, tile_cols:], "wa", 1)
    grad_tile = grads_ext[:tile_rows, :tile_cols].at[:, :BOX].add(from_left)
    return (grad_tile, kernel_grads.reshape(LAYERS, 3, 3, channels, channels))


def solution(mesh):
    in_specs = (
        P("ha", "wa", None),
        P("ha", "wa"),
        P("ha", None),
        P(("ha", "wa"), None),
        P(("ha", "wa"), None),
        P(),
        P(("ha", "wa"), None, None, None),
    )
    out_specs = (P("ha", "wa", None), P())
    return jax.shard_map(local, mesh=mesh, in_specs=in_specs, out_specs=out_specs, check_vma=False)
```

profile of v0, /device:TPU:0, one launch (start us, length us, event | category | flops | bytes accessed | tf_op | source)
XLA Modules:
  0.0 510.1 jit_solution(5376541411540216285)
XLA Ops:
  13.3 11.5 %all-reduce.4 = s32[8]{0:T(128)S(1)} all-reduce(s32[8]{0:T(128)S(1)} %bitcast_dynamic-update-slice_fusion), channel_id=1, replica_groups=mesh['ha'=4,'wa'=8] {'wa'}, use_global_device_ids=true, to_apply=%add.4 | all-reduce | flops 8 | bytes 64 | tf_op jit(solution)/shard_map/squeeze | solution.py:104
  42.6 11.6 %all-to-all-done = bf16[8,2,50176]{2,1,0:T(2,128)(2,1)S(1)} async-done(((bf16[8,2,50176]{2,1,0:T(2,128)(2,1)}), bf16[8,2,50176]{2,1,0:T(2,128)(2,1)S(1)}, u32[]{:S(2)}, u32[]{:S(2)}) %all-to-all-start) | async-done | bytes 1605664 | tf_op jit(solution)/shard_map/all_to_all | solution.py:138
  55.7 3.7 fusion
  59.5 3.7 reshape.997
  67.7 20.1 %convert_bitcast_fusion = bf16[16,14,14,256]{3,2,1,0:T(8,128)(2,1)S(1)} fusion(f32[16,14,64,256]{3,0,2,1:T(8,128)S(1)} %fusion.56, f32[16,14,64,1]{2,0,1,3:T(8,128)S(1)} %maximum_bitcast_fusion.2), kind=kOutput, calls=%fused_computation.116 | convolution fusion | flops 617365504 | bytes 16343040 | tf_op jit(solution)/shard_map/sjx,sixc->sijc/dot_general | solution.py:101
  104.9 21.7 %reshape.970 = bf16[3136,2304]{1,0:T(8,128)(2,1)} reshape(bf16[16,14,14,2304]{3,2,1,0:T(8,128)(2,1)} %slice_dynamic-update-slice_fusion) | data formatting | bytes 28901376 | tf_op jit(solution)/shard_map/reshape | solution.py:37
  126.6 15.4 %multiply_convert_fusion = (bf16[3136,256]{1,0:T(8,128)(2,1)S(1)}, f32[3136,256]{1,0:T(8,128)}, f32[3136,256]{1,0:T(8,128)}) fusion(bf16[3136,2304]{1,0:T(8,128)(2,1)} %reshape.970, bf16[2304,256]{1,0:T(8,128)(2,1)} %bitcast.198), kind=kOutput, calls=%fused_computation.84 | convolution fusion | flops 3751559168 | bytes 23658496 | tf_op jit(solution)/shard_map/dot_general | solution.py:59
  144.6 11.5 %pad_slice_fusion = (bf16[16,14,14,256]{3,2,1,0:T(8,128)(2,1)}, bf16[16,14,14,256]{3,2,1,0:T(8,128)(2,1)}, bf16[16,14,14,256]{3,2,1,0:T(8,128)(2,1)}, bf16[16,14...) fusion(bf16[16,14,14,256]{3,2,1,0:T(8,128)(2,1)} %reshape.971), kind=kLoop, calls=%fused_computation.123 | loop fusion | bytes 14450688 | tf_op jit(solution)/shard_map/slice | solution.py:36
  156.1 3.7 concatenate.87
  159.7 3.6 concatenate.81
  163.4 3.6 concatenate.82
  170.7 4.0 concatenate.84
  174.7 3.7 concatenate.85
  178.4 3.7 concatenate.86
  192.3 11.2 %fusion.10 = bf16[3136,256]{1,0:T(8,128)(2,1)S(1)} fusion(f32[3136,256]{1,0:T(8,128)S(1)} %copy-done.16, bf16[3136,2304]{1,0:T(8,128)(2,1)S(1)} %constant_dynamic-update-slice_fusion.3, bf16[2304,256]{1,0:T(8,128)(2,1)S(1)} %bitcast.201), kind=kOutput, calls=%fused_computation.20 | convolution fusion | flops 3757178880 | bytes 20447232 | tf_op jit(solution)/shard_map/dot_general | solution.py:59
  204.7 6.0 %convolution_bitcast_fusion.1 = f32[1,2304,256]{2,1,0:T(8,128)} fusion(bf16[3136,2304]{1,0:T(8,128)(2,1)S(1)} %constant_dynamic-update-slice_fusion.3, bf16[3136,256]{1,0:T(8,128)(2,1)S(1)} %fusion.10), kind=kOutput, calls=%fused_computation.13 | convolution fusion | flops 3699376128 | bytes 18415616 | tf_op jit(solution)/shard_map/dot_general | solution.py:69
  213.1 13.2 %fusion.65 = f32[16,14,14,9,256]{4,0,3,2,1:T(8,128)} fusion(bf16[9,256,256,1,1]{2,1,0,4,3:T(8,128)(2,1)} %bitcast.200, bf16[16,14,14,256,1]{3,2,1,0,4:T(8,128)(2,1)S(1)} %bitcast.197), kind=kOutput, calls=%fused_computation.120 | convolution fusion | flops 3699376128 | bytes 31686656 | tf_op jit(solution)/shard_map/dot_general | solution.py:73
  229.2 5.3 %fusion.40 = f32[16,16,16,256]{3,0,2,1:T(8,128)S(1)} fusion(f32[16,16,16,256]{3,0,2,1:T(8,128)S(1)} %scatter-add.60, s32[]{:T(128)} %bitcast.25, s32[]{:T(128)} %bitcast.26, f32[16,14,14,9,256]{4,0,3,2,1:T(8,128)} %fusion.65), kind=kLoop, calls=%fused_computation.69 | loop fusion | flops 802816 | bytes 9633800 | tf_op jit(solution)/shard_map/scatter-add | solution.py:46
  234.6 5.8 %fusion.11 = f32[16,16,16,256]{3,0,2,1:T(8,128)S(1)} fusion(f32[16,16,16,256]{3,0,2,1:T(8,128)S(1)} %fusion.40, s32[]{:T(128)} %bitcast.28, s32[]{:T(128)} %bitcast.29, f32[16,14,14,9,256]{4,0,3,2,1:T(8,128)} %fusion.65, pred[]{:T(512)} %and_reduce_fusion), kind=kLoop, calls=%fused_computation.21 | loop fusion | flops 1605632 | bytes 9633801 | tf_op jit(solution)/shard_map/scatter-add | solution.py:46
  245.8 3.7 copy.72
  249.5 4.6 reshape.998
  254.1 6.3 %add_convert_fusion = bf16[3136,256]{1,0:T(8,128)(2,1)} fusion(f32[3136,256]{1,0:T(8,128)} %reshape.998, f32[3136,256]{1,0:T(8,128)} %get-tuple-element.259, f32[3136,256]{1,0:T(8,128)} %get-tuple-element.282), kind=kLoop, calls=%fused_computation.71 | loop fusion | flops 11239424 | bytes 11239424 | tf_op jit(solution)/shard_map/convert_element_type | solution.py:68
  262.8 13.5 %fusion.63 = f32[16,14,14,9,256]{4,0,2,1,3:T(8,128)} fusion(bf16[9,256,256,1,1]{2,1,4,3,0:T(8,128)(2,1)} %bitcast.199, bf16[16,14,14,256]{3,2,1,0:T(8,128)(2,1)S(1)} %dot_general.53), kind=kOutput, calls=%fused_computation.118 | convolution fusion | flops 3699376128 | bytes 31686656 | tf_op jit(solution)/shard_map/dot_general | solution.py:73
  279.2 5.3 %fusion.26 = f32[16,16,16,256]{3,0,2,1:T(8,128)S(1)} fusion(f32[16,16,16,256]{3,0,2,1:T(8,128)S(1)} %scatter-add.75, s32[]{:T(128)} %bitcast.25, s32[]{:T(128)} %bitcast.26, f32[16,14,14,9,256]{4,0,2,1,3:T(8,128)} %fusion.63), kind=kLoop, calls=%fused_computation.45 | loop fusion | flops 802816 | bytes 9633800 | tf_op jit(solution)/shard_map/scatter-add | solution.py:46
  284.5 5.7 %fusion.12 = f32[16,16,16,256]{3,0,2,1:T(8,128)S(1)} fusion(f32[16,16,16,256]{3,0,2,1:T(8,128)S(1)} %fusion.26, s32[]{:T(128)} %bitcast.28, s32[]{:T(128)} %bitcast.29, f32[16,14,14,9,256]{4,0,2,1,3:T(8,128)} %fusion.63, pred[]{:T(512)} %and_reduce_fusion), kind=kLoop, calls=%fused_computation.22 | loop fusion | flops 1605632 | bytes 9633801 | tf_op jit(solution)/shard_map/scatter-add | solution.py:46
  296.2 6.2 %convolution_bitcast_fusion = f32[16,14,64,256]{3,2,1,0:T(8,128)S(1)} fusion(bf16[16,14,14,256]{3,0,2,1:T(8,128)(2,1)S(1)} %slice.993, f32[16,14,64,1]{2,0,1,3:T(8,128)S(1)} %copy-done.18), kind=kOutput, calls=%fused_computation.7 | convolution fusion | flops 616562688 | bytes 16343040 | tf_op jit(solution)/shard_map/sjx,sijc->sixc/dot_general | solution.py:145
  302.4 17.7 %fusion.53 = f32[64,64,256]{2,0,1:T(8,128)S(1)} fusion(f32[16,14,64,256]{3,2,1,0:T(8,128)S(1)} %convolution_bitcast_fusion, s32[16,14]{0,1:T(8,128)S(1)} %copy-done.24, s32[16,64]{1,0:T(8,128)S(1)} %copy-done.22), kind=kOutput, calls=%fused_computation.101 | convolution fusion | flops 2818658304 | bytes 18879360 | tf_op jit(solution)/shard_map/siy,sixc->yxc/dot_general | solution.py:148
  321.6 3.9 collective-permute-start.2
  325.5 7.7 %convolution_bitcast_fusion.2 = f32[1,2304,256]{2,1,0:T(8,128)S(1)} fusion(bf16[3136,2304]{1,0:T(8,128)(2,1)} %reshape.970, bf16[3136,256]{1,0:T(8,128)(2,1)S(1)} %copy-done.14), kind=kOutput, calls=%fused_computation.14 | convolution fusion | flops 3699376128 | bytes 18415616 | tf_op jit(solution)/shard_map/dot_general | solution.py:69
  335.7 56.6 %collective-permute-done.2 = f32[32,64,256]{2,0,1:T(8,128)S(1)} collective-permute-done((f32[32,64,256]{2,0,1:T(8,128)}, f32[32,64,256]{2,0,1:T(8,128)S(1)}, u32[]{:S(2)}, u32[]{:S(2)}) %collective-permute-start.2) | collective-permute-done | bytes 2097184 | tf_op jit(solution)/shard_map/ppermute | solution.py:17
  400.0 98.0 %all-reduce.7.cloned.1.call-done = f32[2,3,3,256,256]{4,3,2,1,0:T(8,128)} async-done(((f32[2,3,3,256,256]{4,3,2,1,0:T(8,128)}), f32[2,3,3,256,256]{4,3,2,1,0:T(8,128)}) %all-reduce.7.cloned.1.call-update) | async-done | bytes 4718608 | tf_op jit(solution)/shard_map/psum | solution.py:143
  498.1 4.9 copy.167
  (147 shorter events, 97.5 us)
Async XLA Ops:
  7.2 19.9 %copy-start = (bf16[8,14,14,256]{3,0,2,1:T(8,128)(2,1)S(1)}, bf16[8,14,14,256]{3,0,2,1:T(8,128)(2,1)}, u32[]{:S(2)}) copy-start(bf16[8,14,14,256]{3,0,2,1:T(8,128)(2,1)} %param.55) | copy-start | bytes 2408452
  9.4 26.4 %collective-permute-start = (bf16[32,32,256]{2,0,1:T(8,128)(2,1)}, bf16[32,32,256]{2,0,1:T(8,128)(2,1)}, u32[]{:S(2)}, u32[]{:S(2)}) collective-permute-start(bf16[32,32,256]{2,0,1:T(8,128)(2,1)} %get-tuple-element.272), channel_id=1, source_target_pairs={{1,0},{2,1},{3,2},{4,3},{5,4},{6,5},{7,6},{9,8},{10,9},{11,10},{12... | collective-permute-start | bytes 1572872 | tf_op jit(solution)/shard_map/ppermute | solution.py:17
  27.7 6.6 %copy-start.28 = (s32[1,8]{1,0:T(1,128)S(1)}, s32[1,8]{1,0:T(1,128)}, u32[]{:S(2)}) copy-start(s32[1,8]{1,0:T(1,128)} %param.51) | copy-start | bytes 100
  27.7 7.4 %copy-start.26 = (s32[16,2]{0,1:T(2,128)S(1)}, s32[16,2]{0,1:T(2,128)}, u32[]{:S(2)}) copy-start(s32[16,2]{0,1:T(2,128)} %param.52) | copy-start | bytes 388
  27.7 8.0 %copy-start.25 = (s32[16,28]{1,0:T(8,128)S(1)}, s32[16,28]{1,0:T(8,128)}, u32[]{:S(2)}) copy-start(s32[16,28]{1,0:T(8,128)} %param.53) | copy-start | bytes 5380
  27.7 10.6 %copy-start.27 = (s32[4]{0:T(128)S(1)}, s32[4]{0:T(128)}, u32[]{:S(2)}) copy-start(s32[4]{0:T(128)} %constant.656.clone.1) | copy-start | bytes 52
  29.3 24.9 %all-to-all-start = ((bf16[8,2,50176]{2,1,0:T(2,128)(2,1)}), bf16[8,2,50176]{2,1,0:T(2,128)(2,1)S(1)}, u32[]{:S(2)}, u32[]{:S(2)}) async-start(bf16[8,2,50176]{2,1,0:T(2,128)(2,1)} %all_to_all.8), calls=%async_computation | async-start | bytes 3211264 | tf_op jit(solution)/shard_map/all_to_all | solution.py:138
  32.9 465.2 %all-reduce.7.cloned.1.call-start = ((), (), s32[]{:S(2)}) async-start(), calls=%async_computation.1 | async-start | bytes 9437184 | tf_op jit(solution)/shard_map/psum | solution.py:143
  35.7 28.6 %copy-start.21 = (s32[16,64]{1,0:T(8,128)}, s32[16,64]{1,0:T(8,128)S(1)}, u32[]{:S(2)}) copy-start(s32[16,64]{1,0:T(8,128)S(1)} %get-tuple-element.284) | copy-start | bytes 12292
  36.9 27.4 %collective-permute-start.1 = (bf16[32,64,256]{2,0,1:T(8,128)(2,1)S(1)}, bf16[32,64,256]{2,0,1:T(8,128)(2,1)}, u32[]{:S(2)}, u32[]{:S(2)}) collective-permute-start(bf16[32,64,256]{2,0,1:T(8,128)(2,1)S(1)} %constant_dynamic-update-slice_fusion), channel_id=1, source_target_pairs={{8,0},{16,8},{24,16},{9,1},{17,9},{25,17},{10,2},{18,10},{26,18},{... | collective-permute-start | bytes 3145736 | tf_op jit(solution)/shard_map/ppermute | solution.py:17
  38.4 25.9 %copy-start.23 = (s32[16,14]{0,1:T(8,128)}, s32[16,14]{0,1:T(8,128)S(1)}, u32[]{:S(2)}) copy-start(s32[16,14]{0,1:T(8,128)S(1)} %copy.57) | copy-start | bytes 2692
  39.3 28.4 %copy-start.17 = (f32[16,14,64,1]{2,0,1,3:T(8,128)}, f32[16,14,64,1]{2,0,1,3:T(8,128)S(1)}, u32[]{:S(2)}) copy-start(f32[16,14,64,1]{2,0,1,3:T(8,128)S(1)} %maximum_bitcast_fusion.2) | copy-start | bytes 172036
  183.4 1.9 copy-start.13
  183.4 2.4 copy-start.12
  185.3 1.5 copy-start.11
  185.8 1.5 copy-start.6
  186.9 1.5 copy-start.10
  187.3 1.5 copy-start.9
  188.4 1.5 copy-start.8
  188.9 1.5 copy-start.7
  189.9 1.4 copy-start.15
  190.0 2.4 copy-start.16
  226.3 14.0 %copy-start.2 = (f32[16,14,14,9,256]{4,0,3,2,1:T(8,128)S(1)}, f32[16,14,14,9,256]{4,0,3,2,1:T(8,128)}, u32[]{:S(2)}) copy-start(f32[16,14,14,9,256]{4,0,3,2,1:T(8,128)} %fusion.65) | copy-start | bytes 86704128
  276.3 13.9 %copy-start.3 = (f32[16,14,14,9,256]{4,0,2,1,3:T(8,128)S(1)}, f32[16,14,14,9,256]{4,0,2,1,3:T(8,128)}, u32[]{:S(2)}) copy-start(f32[16,14,14,9,256]{4,0,2,1,3:T(8,128)} %fusion.63) | copy-start | bytes 86704128
  296.2 6.2 %copy-start.22 = (s32[16,64]{1,0:T(8,128)S(1)}, s32[16,64]{1,0:T(8,128)}, u32[]{:S(2)}) copy-start(s32[16,64]{1,0:T(8,128)} %copy-done.21) | copy-start | bytes 12292
  296.2 6.2 %copy-start.24 = (s32[16,14]{0,1:T(8,128)S(1)}, s32[16,14]{0,1:T(8,128)}, u32[]{:S(2)}) copy-start(s32[16,14]{0,1:T(8,128)} %copy-done.23) | copy-start | bytes 2692
  320.1 13.0 %copy-start.4 = (f32[64,64,256]{2,0,1:T(8,128)}, f32[64,64,256]{2,0,1:T(8,128)S(1)}, u32[]{:S(2)}) copy-start(f32[64,64,256]{2,0,1:T(8,128)S(1)} %fusion.53) | copy-start | bytes 12582916
  320.1 5.3 %copy-start.14 = (bf16[3136,256]{1,0:T(8,128)(2,1)S(1)}, bf16[3136,256]{1,0:T(8,128)(2,1)}, u32[]{:S(2)}) copy-start(bf16[3136,256]{1,0:T(8,128)(2,1)} %add_convert_fusion) | copy-start | bytes 4816900
  321.6 11.6 %copy-start.19 = (f32[1,2304,256]{2,1,0:T(8,128)S(1)}, f32[1,2304,256]{2,1,0:T(8,128)}, u32[]{:S(2)}) copy-start(f32[1,2304,256]{2,1,0:T(8,128)} %convolution_bitcast_fusion.1) | copy-start | bytes 7077892
  321.6 70.8 %collective-permute-start.2 = (f32[32,64,256]{2,0,1:T(8,128)}, f32[32,64,256]{2,0,1:T(8,128)S(1)}, u32[]{:S(2)}, u32[]{:S(2)}) collective-permute-start(f32[32,64,256]{2,0,1:T(8,128)} %slice.876), channel_id=1, source_target_pairs={{0,8},{8,16},{16,24},{1,9},{9,17},{17,25},{2,10},{10,18},{18,26},{... | collective-permute-start | bytes 6291464 | tf_op jit(solution)/shard_map/ppermute | solution.py:17
  394.7 3.6 collective-permute-start.3
  398.4 104.6 %copy-start.1 = (bf16[8,14,14,256]{3,0,2,1:T(8,128)(2,1)S(1)}, bf16[8,14,14,256]{3,0,2,1:T(8,128)(2,1)}, u32[]{:S(2)}) copy-start(bf16[8,14,14,256]{3,0,2,1:T(8,128)(2,1)} %param.55) | copy-start | bytes 2408452
  (3 other events, 3.3 us)
Sparse Core Ops, SparseCore 0:
  335.8 162.1 all-reduce.6
where the time goes:
time: 516 us; the launch traced here: 510 us
  waiting for transfers between devices  170 us (33%)
  local copies, waits for them, and re-layouts  135 us (26%)
  matrix products  119 us (23%)
  other arithmetic  48.3 us (9%)
  between operations  15.5 us (3%)
  blocking collectives  11.5 us (2%)
  starting transfers between devices  11.4 us (2%)
    psum x1, waiting for transfers between devices, local(): kernel_grads = lax.psum(kernel_grads, ('ha', 'wa'))  98 us
    ppermute x4, waiting for transfers between devices, shifted(): lax.ppermute(value, axis, [(source, source + steps) for source in range(f...  59.9 us
    unnamed x80, local copies, waits for them, and re-layouts  37.7 us
    scatter-add x16, other arithmetic, fold_back(): totals.at[:, row_step:row_step + SIDE, col_step:col_step + SIDE, :]  32.1 us
    concatenate x10, local copies, waits for them, and re-layouts, patches_of(): jnp.concatenate(pieces, axis=3).reshape(amount * SIDE * SIDE, 9 * channels)  29.4 us
    dot_general x2, matrix products, mask_head(): lax.dot_general(inner_grad, matrix, (((1,), (1,)), ((), ())), preferred_e...  26.7 us
    dot_general x2, matrix products, mask_head(): before = jnp.dot(columns, matrix, preferred_element_type=jnp.float32)  26.6 us
    reshape x1, local copies, waits for them, and re-layouts, patches_of(): jnp.concatenate(pieces, axis=3).reshape(amount * SIDE * SIDE, 9 * channels)  21.7 us
  transfers between devices with their start and end apart: 6, of which 5 were waited for; matrix products, arithmetic and copies ran while one was open for 7% of the time, Pallas kernels for 0%

commit v1 on v0

v1 whole, which is shorter than its diff:
```python
import jax
import jax.numpy as jnp
from jax import lax
from jax.experimental import pallas as pl
from jax.experimental.pallas import tpu as pltpu
from jax.sharding import PartitionSpec as P

SIDE = 14
BOX = 32
LAYERS = 2
GRID = 16
CELLS = GRID * GRID
FAR = 4096.0
VMEM_BYTES = 56 * 2**20


def shifted(value, steps_ha, steps_wa):
    rows, cols = lax.axis_size("ha"), lax.axis_size("wa")
    pairs = []
    for row in range(rows):
        for col in range(cols):
            to_row, to_col = row + steps_ha, col + steps_wa
            if 0 <= to_row < rows and 0 <= to_col < cols:
                pairs.append((row * cols + col, to_row * cols + to_col))
    return lax.ppermute(value, ("ha", "wa"), pairs)


def gelu_and_slope(v):
    phi = 0.5 * (1.0 + lax.erf(v * 0.7071067811865476))
    slope = phi + v * (0.3989422804014327 * jnp.exp(-0.5 * v * v))
    return v * phi, slope


def cell_mask(rows, channels):
    at = lax.broadcasted_iota(jnp.int32, (rows, channels), 0)
    return jnp.logical_and(at % GRID < SIDE, (at // GRID) % GRID < SIDE)


def fill_shifts(ref, value, sign):
    rows, channels = value.shape
    zero = jnp.zeros((GRID, 3 * channels), jnp.bfloat16)
    ref[0:GRID, :] = zero
    ref[GRID + rows : 2 * GRID + rows, :] = zero
    for d in range(3):
        steps = (-sign * (d - 1)) % rows
        moved = pltpu.roll(value, steps, 0) if steps else value
        ref[GRID : GRID + rows, d * channels : (d + 1) * channels] = moved.astype(jnp.bfloat16)


def forward_kernel(
    tops, ext_ref, row_ref, col_ref, w_ref, x0t_ref, x1t_ref, s0_ref, s1_ref, mix, stack, value
):
    group = row_ref.shape[0] // CELLS
    rows = group * CELLS
    span, channels = ext_ref.shape[1], ext_ref.shape[2]
    step = pl.program_id(0)
    lane = lax.broadcasted_iota(jnp.int32, (CELLS, 2 * span), 1)
    upper = (lane >= span).astype(jnp.float32)
    across = (lane % span).astype(jnp.float32)
    for s in range(group):
        here = slice(s * CELLS, (s + 1) * CELLS)
        reach = jnp.maximum(0.0, 1.0 - jnp.abs(across - col_ref[here, :]))
        away = upper - row_ref[here, :]
        for k in range(BOX // 2):
            weight = jnp.maximum(0.0, 1.0 - jnp.abs(away + float(2 * k)))
            mix[:, k * 2 * span : (k + 1) * 2 * span] = (weight * reach).astype(jnp.bfloat16)
        top = tops[step * group + s]
        window = ext_ref[pl.ds(top, BOX)].reshape(BOX * span, channels)
        value[here, :] = jnp.dot(mix[...], window, preferred_element_type=jnp.float32)
    keep = cell_mask(rows, channels)

    def conv(layer):
        total = jnp.dot(stack[0:rows, :], w_ref[layer, 0], preferred_element_type=jnp.float32)
        for dy in range(1, 3):
            total += jnp.dot(
                stack[dy * GRID : dy * GRID + rows, :],
                w_ref[layer, dy],
                preferred_element_type=jnp.float32,
            )
        return total

    samples = value[...]
    x0t_ref[...] = samples.T.astype(jnp.bfloat16)
    fill_shifts(stack, samples, 1)
    act, slope = gelu_and_slope(conv(0))
    s0_ref[...] = jnp.where(keep, slope, 0.0)
    act = jnp.where(keep, act, 0.0)
    x1t_ref[...] = act.T.astype(jnp.bfloat16)
    fill_shifts(stack, act, 1)
    _, slope = gelu_and_slope(conv(1))
    s1_ref[...] = slope


def add_kernel_grads(g_ref, xt_ref, stack):
    rows = xt_ref.shape[1]
    channels = xt_ref.shape[0]

    @pl.when(pl.program_id(0) == 0)
    def _():
        g_ref[...] = jnp.zeros_like(g_ref)

    xt = xt_ref[...]
    for dy in range(3):
        for dx in range(3):
            g_ref[dy, dx] += jnp.dot(
                xt,
                stack[2 * GRID - dy * GRID : 2 * GRID - dy * GRID + rows, dx * channels : (dx + 1) * channels],
                preferred_element_type=jnp.float32,
            )


def back_through(wt_ref, stack, rows):
    total = jnp.dot(stack[2 * GRID : 2 * GRID + rows, :], wt_ref[0], preferred_element_type=jnp.float32)
    for dy in range(1, 3):
        total += jnp.dot(
            stack[2 * GRID - dy * GRID : 2 * GRID - dy * GRID + rows, :],
            wt_ref[dy],
            preferred_element_type=jnp.float32,
        )
    return total


def top_layer_kernel(route, inc_ref, s1_ref, s0_ref, x1t_ref, wt_ref, g_ref, pg_ref, stack, value):
    rows, channels = s1_ref.shape
    group = rows // CELLS
    used = inc_ref.shape[1]
    step = pl.program_id(0)
    for s in range(group):
        slot = step * group + s
        live = route[1, slot].astype(jnp.float32)
        value[s * CELLS : s * CELLS + used, :] = inc_ref[route[0, slot]].astype(jnp.float32) * live
        value[s * CELLS + used : (s + 1) * CELLS, :] = jnp.zeros((CELLS - used, channels), jnp.float32)
    fill_shifts(stack, value[...] * s1_ref[...], -1)
    add_kernel_grads(g_ref, x1t_ref, stack)
    grad = back_through(wt_ref, stack, rows)
    pg_ref[...] = (grad.astype(jnp.bfloat16).astype(jnp.float32) * s0_ref[...]).astype(jnp.bfloat16)


def low_grads_kernel(pg_ref, x0t_ref, g_ref, stack):
    fill_shifts(stack, pg_ref[...].astype(jnp.float32), -1)
    add_kernel_grads(g_ref, x0t_ref, stack)


def spread_kernel(tops, pg_ref, place_ref, wt_ref, out_ref, stack, value):
    rows, channels = pg_ref.shape
    group = rows // CELLS
    span = out_ref.shape[1]
    part = 8
    step = pl.program_id(0)

    @pl.when(step == 0)
    def _():
        out_ref[...] = jnp.zeros_like(out_ref)

    fill_shifts(stack, pg_ref[...].astype(jnp.float32), -1)
    value[...] = back_through(wt_ref, stack, rows).astype(jnp.bfloat16)
    across = lax.broadcasted_iota(jnp.int32, (span, CELLS), 0).astype(jnp.float32)
    for s in range(group):
        row_at = place_ref[s, 0:1, :]
        col_at = place_ref[s, 1:2, :]
        reach = jnp.maximum(0.0, 1.0 - jnp.abs(across - col_at))
        grad = value[s * CELLS : (s + 1) * CELLS, :]
        top = tops[step * group + s]
        for k in range(BOX // part):
            pieces = []
            for p in range(part):
                weight = jnp.maximum(0.0, 1.0 - jnp.abs(float(k * part + p) - row_at))
                pieces.append((weight * reach).astype(jnp.bfloat16))
            mixed = jnp.concatenate(pieces, axis=0)
            spread = jnp.dot(mixed, grad, preferred_element_type=jnp.float32)
            out_ref[pl.ds(top + k * part, part)] += spread.reshape(part, span, channels)


def pick_kernel(index, in_ref, out_ref):
    out_ref[...] = in_ref[...]


def params():
    return pltpu.CompilerParams(vmem_limit_bytes=VMEM_BYTES)


def cost(flops, nbytes, exps=0):
    return pl.CostEstimate(flops=flops, bytes_accessed=nbytes, transcendentals=exps)


def local(features, counts, owner_perm, corners, offsets, kernels, cotangent):
    tile_rows, tile_cols, channels = features.shape
    slot_total = corners.shape[0]
    owned = cotangent.shape[0]
    width_count = lax.axis_size("wa")
    pairs = slot_total // width_count
    col_index = lax.axis_index("wa")
    group = 4 if slot_total % 4 == 0 else 1
    steps = slot_total // group
    rows = group * CELLS
    all_rows = slot_total * CELLS
    span = tile_cols + BOX

    right_edge = shifted(features, 0, -1)
    lower_edge = shifted(features, -1, 0)
    corner_edge = shifted(features, -1, -1)

    row_counts = lax.all_gather(counts, "wa", axis=1, tiled=True)[0]
    starts = jnp.cumsum(row_counts) - row_counts
    device_ids = jnp.arange(width_count, dtype=jnp.int32)
    here_start = jnp.sum(jnp.where(device_ids == col_index, starts, 0))
    perm_row = owner_perm[0]
    slot_ids = jnp.arange(slot_total, dtype=jnp.int32)
    stream = here_start + slot_ids
    owner_of = jnp.sum(
        jnp.where((stream % width_count)[:, None] == device_ids[None, :], perm_row[None, :], 0),
        axis=1,
    )
    live_slot = (slot_ids < counts[0, 0]).astype(jnp.int32)
    route = jnp.stack([owner_of * pairs + slot_ids // width_count, live_slot])
    buffer_ids = jnp.arange(width_count * pairs, dtype=jnp.int32)
    position = jnp.sum(jnp.where(perm_row == col_index, device_ids, 0))
    sender_match = (buffer_ids // pairs)[:, None] == device_ids[None, :]
    sender_start = jnp.sum(jnp.where(sender_match, starts[None, :], 0), axis=1)
    arrival = (
        sender_start + (position - sender_start) % width_count + buffer_ids % pairs * width_count
    )
    chosen = jnp.clip(arrival // width_count, 0, owned - 1)
    padded = jnp.pad(cotangent, ((0, 0), (0, 0), (0, GRID - SIDE), (0, 0)))
    padded = padded.reshape(owned, SIDE * GRID, channels)
    block = (1, SIDE * GRID, channels)
    outgoing = pl.pallas_call(
        pick_kernel,
        out_shape=jax.ShapeDtypeStruct((width_count * pairs,) + block[1:], jnp.bfloat16),
        grid_spec=pltpu.PrefetchScalarGridSpec(
            num_scalar_prefetch=1,
            grid=(width_count * pairs,),
            in_specs=[pl.BlockSpec(block, lambda b, index: (index[b], 0, 0))],
            out_specs=pl.BlockSpec(block, lambda b, index: (b, 0, 0)),
        ),
    )(chosen, padded)
    incoming = lax.all_to_all(outgoing, "wa", split_axis=0, concat_axis=0, tiled=True)

    fill = ((0, 0), (0, GRID - SIDE))
    row_at = jnp.pad(offsets[:, :SIDE].astype(jnp.float32) * 0.25, fill, constant_values=FAR)
    col_at = offsets[:, SIDE:].astype(jnp.float32) * 0.25 + corners[:, 1:2].astype(jnp.float32)
    col_at = jnp.pad(col_at, fill, constant_values=FAR)
    row_cell = jnp.broadcast_to(row_at[:, :, None], (slot_total, GRID, GRID)).reshape(slot_total, CELLS)
    col_cell = jnp.broadcast_to(col_at[:, None, :], (slot_total, GRID, GRID)).reshape(slot_total, CELLS)
    place = jnp.stack([row_cell, col_cell], axis=1)
    row_wide = jnp.broadcast_to(row_cell.reshape(all_rows, 1), (all_rows, 2 * span))
    col_wide = jnp.broadcast_to(col_cell.reshape(all_rows, 1), (all_rows, 2 * span))
    tops = corners[:, 0]

    extended = jnp.concatenate(
        [
            jnp.concatenate([features, right_edge], axis=1),
            jnp.concatenate([lower_edge, corner_edge], axis=1),
        ],
        axis=0,
    )
    ahead = kernels.reshape(LAYERS, 3, 3 * channels, channels)
    back = kernels.transpose(0, 1, 2, 4, 3).reshape(LAYERS, 3, 3 * channels, channels)
    conv_flops = 2 * all_rows * 9 * channels * channels

    def tall(width):
        return pl.BlockSpec((rows, width), lambda t, *_: (t, 0))

    def wide():
        return pl.BlockSpec((channels, rows), lambda t, *_: (0, t))

    def fixed(shape):
        return pl.BlockSpec(shape, lambda t, *_: (0,) * len(shape))

    f32 = lambda *shape: jax.ShapeDtypeStruct(shape, jnp.float32)
    b16 = lambda *shape: jax.ShapeDtypeStruct(shape, jnp.bfloat16)
    stack_scratch = pltpu.VMEM((rows + 2 * GRID, 3 * channels), jnp.bfloat16)
    value_scratch = pltpu.VMEM((rows, channels), jnp.float32)
    grads_shape = (3, 3, channels, channels)

    x0t, x1t, slope0, slope1 = pl.pallas_call(
        forward_kernel,
        out_shape=(
            b16(channels, all_rows),
            b16(channels, all_rows),
            f32(all_rows, channels),
            f32(all_rows, channels),
        ),
        grid_spec=pltpu.PrefetchScalarGridSpec(
            num_scalar_prefetch=1,
            grid=(steps,),
            in_specs=[fixed(extended.shape), tall(2 * span), tall(2 * span), fixed(ahead.shape)],
            out_specs=(wide(), wide(), tall(channels), tall(channels)),
            scratch_shapes=[
                pltpu.VMEM((CELLS, BOX * span), jnp.bfloat16),
                stack_scratch,
                value_scratch,
            ],
        ),
        compiler_params=params(),
        cost_estimate=cost(2 * conv_flops + 2 * all_rows * BOX * span * channels, 24 * 2**20, 4 * all_rows * channels),
    )(tops, extended, row_wide, col_wide, ahead)

    top_grads, pre_grad = pl.pallas_call(
        top_layer_kernel,
        out_shape=(f32(*grads_shape), b16(all_rows, channels)),
        grid_spec=pltpu.PrefetchScalarGridSpec(
            num_scalar_prefetch=1,
            grid=(steps,),
            in_specs=[
                fixed(incoming.shape),
                tall(channels),
                tall(channels),
                wide(),
                fixed((3, 3 * channels, channels)),
            ],
            out_specs=(fixed(grads_shape), tall(channels)),
            scratch_shapes=[stack_scratch, value_scratch],
        ),
        compiler_params=params(),
        cost_estimate=cost(2 * conv_flops, 16 * 2**20),
    )(route, incoming, slope1, slope0, x1t, back[1])
    top_total = lax.psum(top_grads.astype(jnp.bfloat16), ("ha", "wa"))

    low_grads = pl.pallas_call(
        low_grads_kernel,
        out_shape=f32(*grads_shape),
        grid=(steps,),
        in_specs=[tall(channels), wide()],
        out_specs=fixed(grads_shape),
        scratch_shapes=[stack_scratch],
        compiler_params=params(),
        cost_estimate=cost(conv_flops, 8 * 2**20),
    )(pre_grad, x0t)
    low_total = lax.psum(low_grads.astype(jnp.bfloat16), ("ha", "wa"))

    grads_ext = pl.pallas_call(
        spread_kernel,
        out_shape=f32(tile_rows + BOX, span, channels),
        grid_spec=pltpu.PrefetchScalarGridSpec(
            num_scalar_prefetch=1,
            grid=(steps,),
            in_specs=[
                tall(channels),
                pl.BlockSpec((group, 2, CELLS), lambda t, *_: (t, 0, 0)),
                fixed((3, 3 * channels, channels)),
            ],
            out_specs=fixed((tile_rows + BOX, span, channels)),
            scratch_shapes=[stack_scratch, pltpu.VMEM((rows, channels), jnp.bfloat16)],
        ),
        compiler_params=params(),
        cost_estimate=cost(conv_flops + 2 * all_rows * BOX * span * channels, 8 * 2**20),
    )(tops, pre_grad, place, back[0])
    to_right = grads_ext[:tile_rows, tile_cols:].astype(jnp.bfloat16)
    to_below = grads_ext[tile_rows:, :tile_cols].astype(jnp.bfloat16)
    to_corner = grads_ext[tile_rows:, tile_cols:].astype(jnp.bfloat16)
    from_left = shifted(to_right, 0, 1).astype(jnp.float32)
    from_above = shifted(to_below, 1, 0).astype(jnp.float32)
    from_corner = shifted(to_corner, 1, 1).astype(jnp.float32)
    grad_tile = grads_ext[:tile_rows, :tile_cols]
    grad_tile = grad_tile.at[:, :BOX].add(from_left)
    grad_tile = grad_tile.at[:BOX].add(from_above)
    grad_tile = grad_tile.at[:BOX, :BOX].add(from_corner)
    kernel_grads = jnp.stack([low_total, top_total]).astype(jnp.float32)
    return (grad_tile, kernel_grads)


def solution(mesh):
    in_specs = (
        P("ha", "wa", None),
        P("ha", "wa"),
        P("ha", None),
        P(("ha", "wa"), None),
        P(("ha", "wa"), None),
        P(),
        P(("ha", "wa"), None, None, None),
    )
    out_specs = (P("ha", "wa", None), P())
    return jax.shard_map(local, mesh=mesh, in_specs=in_specs, out_specs=out_specs, check_vma=False)
```

time: 516 us -> 278 us (0.54)
  local copies, waits for them, and re-layouts: 135 us -> 13.7 us
  matrix products: 119 us -> 0 us
  Pallas kernels: 0 us -> 95.9 us
  waiting for transfers between devices: 170 us -> 99.4 us
  other arithmetic: 48.3 us -> 21.3 us
  starting transfers between devices: 11.4 us -> 21.4 us
    dot_general x12 -> x0, matrix products: 119 us -> none  [the longest x2 26.7 us: mask_head(): lax.dot_general(inner_grad, matrix, (((1,), (1,)), ((), ())), preferred_e...]
    pallas_call x0 -> x5, Pallas kernels: none -> 95.9 us  [the longest x1 37.4 us: local(): pl.pallas_call(forward_kernel, out_shape=(b16(channels, all_rows), b16(ch...]
    ppermute x4 -> x6, waiting for transfers between devices: 59.9 us -> 20.6 us  [shifted(): return lax.ppermute(value, ('ha', 'wa'), pairs)]
    unnamed x80 -> x14, local copies, waits for them, and re-layouts: 37.7 us -> 3.25 us
    scatter-add x16 -> x0, other arithmetic: 32.1 us -> none  [fold_back(): totals.at[:, row_step:row_step + SIDE, col_step:col_step + SIDE, :]]
    concatenate x11 -> x0, local copies, waits for them, and re-layouts: 30.5 us -> none  [the longest x10 29.4 us: patches_of(): jnp.concatenate(pieces, axis=3).reshape(amount * SIDE * SIDE, 9 * channels)]
    reshape x2 -> x0, local copies, waits for them, and re-layouts: 23.1 us -> none  [the longest x1 21.7 us: patches_of(): jnp.concatenate(pieces, axis=3).reshape(amount * SIDE * SIDE, 9 * channels)]
    psum x1, waiting for transfers between devices: 98 us -> 78.8 us  [local(): top_total = lax.psum(top_grads.astype(jnp.bfloat16), ('ha', 'wa'))]
  transfers between devices with their start and end apart: 6 -> 8, of which waited for: 5 -> 3; matrix products, arithmetic and copies ran while one was open for 7% -> 10% of each run, Pallas kernels for 0% -> 25%
where the time goes in v1:
time: 278 us; the launch traced here: 277 us
  waiting for transfers between devices  99.4 us (36%)
  Pallas kernels  95.9 us (34%)
  starting transfers between devices  21.4 us (8%)
  other arithmetic  21.3 us (8%)
  between operations  14.9 us (5%)
  local copies, waits for them, and re-layouts  13.7 us (5%)
  blocking collectives  10.3 us (4%)
    psum x1, waiting for transfers between devices, local(): top_total = lax.psum(top_grads.astype(jnp.bfloat16), ('ha', 'wa'))  78.8 us
    pallas_call x1, Pallas kernels, local(): pl.pallas_call(forward_kernel, out_shape=(b16(channels, all_rows), b16(ch...  37.4 us
    pallas_call x1, Pallas kernels, local(): pl.pallas_call(spread_kernel, out_shape=f32(tile_rows + BOX, span, channe...  23 us
    ppermute x6, waiting for transfers between devices, shifted(): return lax.ppermute(value, ('ha', 'wa'), pairs)  20.6 us
    ppermute x6, starting transfers between devices, shifted(): return lax.ppermute(value, ('ha', 'wa'), pairs)  16.9 us
    pallas_call x1, Pallas kernels, local(): pl.pallas_call(top_layer_kernel, out_shape=(f32(*grads_shape), b16(all_ro...  16.4 us
    squeeze x1, blocking collectives, local(): row_counts = lax.all_gather(counts, 'wa', axis=1, tiled=True)[0]  10.3 us
    pallas_call x1, Pallas kernels, local(): pl.pallas_call(pick_kernel, out_shape=jax.ShapeDtypeStruct((width_count *...  9.6 us
  transfers between devices with their start and end apart: 8, of which 3 were waited for; matrix products, arithmetic and copies ran while one was open for 10% of the time, Pallas kernels for 25%

profile of v1, /device:TPU:0, one launch (start us, length us, event | category | flops | bytes accessed | tf_op | source)
XLA Modules:
  0.0 277.0 jit_solution(11668418614704752145)
XLA Ops:
  7.2 1.3 collective-permute-start
  8.5 1.3 collective-permute-start.1
  9.8 1.3 collective-permute-start.2
  11.7 1.2 dynamic-slice.15
  13.0 0.7 bitcast_dynamic-update-slice_fusion
  13.6 10.3 %all-reduce.3 = s32[8]{0:T(128)S(1)} all-reduce(s32[8]{0:T(128)S(1)} %bitcast_dynamic-update-slice_fusion), channel_id=1, replica_groups=mesh['ha'=4,'wa'=8] {'wa'}, use_global_device_ids=true, to_apply=%add.3 | all-reduce | flops 8 | bytes 64 | tf_op jit(solution)/shard_map/squeeze | solution.py:203
  24.2 1.3 copy.15
  25.6 1.3 fusion.7
  26.9 1.2 fusion.11.index
  28.1 1.0 pad.20.clone
  29.1 9.6 %shard_map.101 = bf16[16,224,256]{2,1,0:T(8,128)(2,1)} custom-call(s32[16]{0:T(128)} %fusion.11.index, bf16[8,224,256]{2,1,0:T(8,128)(2,1)} %bitcast.35), custom_call_target="tpu_custom_call" | custom-call | tf_op jit(solution)/shard_map/pallas_call | solution.py:227
  38.7 4.5 %all-to-all-start = ((bf16[16,224,256]{2,1,0:T(8,128)(2,1)}), bf16[16,224,256]{2,1,0:T(8,128)(2,1)}, u32[]{:S(2)}, u32[]{:S(2)}) async-start(bf16[16,224,256]{2,1,0:T(8,128)(2,1)} %shard_map.101), calls=%async_computation | async-start | bytes 3670016 | tf_op jit(solution)/shard_map/all_to_all | solution.py:237
  45.7 1.8 fusion.12
  47.5 1.6 copy.13
  49.1 1.5 copy.14
  52.0 2.7 maximum_maximum_fusion.ext_ref
  54.7 1.9 broadcast_in_dim.66.row_ref
  56.7 1.9 broadcast_in_dim.69.col_ref
  58.6 37.4 %shard_map.102 = (bf16[256,4096]{1,0:T(8,128)(2,1)}, bf16[256,4096]{1,0:T(8,128)(2,1)}, f32[4096,256]{1,0:T(8,128)}, f32[4096,256]{1,0:T(8,128)}) custom-call(s32[16]{0:T(128)} %get-tuple-element.84.tops, bf16[64,64,256]{2,1,0:T(8,128)(2,1)} %maximum_maximum_fusion.ext_ref, f32[4096,128]{1,0:T(8,128)} %broadcast_in_dim.66.row_ref, ...), custom_call_target="tpu_custom_call" | custom-call | flops 13958643712 | bytes 25165824 | tf_op jit(solution)/shard_map/pallas_call | solution.py:276
  96.0 16.4 %shard_map.103 = (f32[3,3,256,256]{3,2,1,0:T(8,128)}, bf16[4096,256]{1,0:T(8,128)(2,1)}) custom-call(s32[2,16]{1,0:T(2,128)} %pad_add_fusion.route, bf16[16,224,256]{2,1,0:T(8,128)(2,1)} %all-to-all-done.inc_ref, f32[4096,256]{1,0:T(8,128)} %get-tuple-element.68.s1_ref, f32[4096,256]{1,0:T(8,128)} %get-tuple-element.69.s0_ref, ...), custom_call_target="tpu_custom_call" | custom-call | flops 9663676416 | bytes 16777216 | tf_op jit(solution)/shard_map/pallas_call | solution.py:299
  112.4 9.5 %shard_map.105 = f32[3,3,256,256]{3,2,1,0:T(8,128)} custom-call(bf16[4096,256]{1,0:T(8,128)(2,1)} %get-tuple-element.71.pg_ref, bf16[256,4096]{1,0:T(8,128)(2,1)} %get-tuple-element.72.x0t_ref), custom_call_target="tpu_custom_call" | custom-call | flops 4831838208 | bytes 8388608 | tf_op jit(solution)/shard_map/pallas_call | solution.py:320
  122.0 3.4 %convert_bitcast_fusion = (bf16[1,3,3,256,256]{4,3,2,1,0:T(8,128)(2,1)}, bf16[1,3,3,256,256]{4,3,2,1,0:T(8,128)(2,1)}) fusion(f32[3,3,256,256]{3,2,1,0:T(8,128)S(1)} %copy-done, f32[3,3,256,256]{3,2,1,0:T(8,128)} %shard_map.105), kind=kLoop, calls=%fused_computation.2 | loop fusion | flops 1179648 | bytes 7077888 | tf_op jit(solution)/shard_map/stack | solution.py:359
  125.4 23.0 %shard_map.104 = f32[64,64,256]{2,1,0:T(8,128)} custom-call(s32[16]{0:T(128)} %get-tuple-element.84.tops, bf16[4096,256]{1,0:T(8,128)(2,1)} %get-tuple-element.71.pg_ref, f32[16,2,256]{2,1,0:T(2,128)} %pad_maximum_fusion.place_ref, bf16[3,768,256]{2,1,0:T(8,128)(2,1)} %bitcast.38), custom_call_target="tpu_custom_call" | custom-call | flops 9126805504 | bytes 8388608 | tf_op jit(solution)/shard_map/pallas_call | solution.py:332
  148.4 2.5 convert.5
  151.0 2.3 collective-permute-start.3
  153.3 5.7 %collective-permute-start.4 = (bf16[32,32,256]{2,1,0:T(8,128)(2,1)S(1)}, bf16[32,32,256]{2,1,0:T(8,128)(2,1)S(1)}, u32[]{:S(2)}, u32[]{:S(2)}) collective-permute-start(bf16[32,32,256]{2,1,0:T(8,128)(2,1)S(1)} %get-tuple-element.80), channel_id=1, source_target_pairs={{0,8},{1,9},{2,10},{3,11},{4,12},{5,13},{6,14},{7,15},{8,16},{9,17... | collective-permute-start | bytes 1572872 | tf_op jit(solution)/shard_map/ppermute | solution.py:25
  159.0 5.1 %collective-permute-start.5 = (bf16[32,32,256]{2,1,0:T(8,128)(2,1)S(1)}, bf16[32,32,256]{2,1,0:T(8,128)(2,1)S(1)}, u32[]{:S(2)}, u32[]{:S(2)}) collective-permute-start(bf16[32,32,256]{2,1,0:T(8,128)(2,1)S(1)} %get-tuple-element.79), channel_id=1, source_target_pairs={{0,9},{1,10},{2,11},{3,12},{4,13},{5,14},{6,15},{8,17},{9,18},{10,... | collective-permute-start | bytes 1572872 | tf_op jit(solution)/shard_map/ppermute | solution.py:25
  164.1 7.8 %collective-permute-done.4 = bf16[32,32,256]{2,1,0:T(8,128)(2,1)S(1)} collective-permute-done((bf16[32,32,256]{2,1,0:T(8,128)(2,1)S(1)}, bf16[32,32,256]{2,1,0:T(8,128)(2,1)S(1)}, u32[]{:S(2)}, u32[]{:S(2)}) %collective-permute-start.4) | collective-permute-done | bytes 524320 | tf_op jit(solution)/shard_map/ppermute | solution.py:25
  171.8 12.8 %collective-permute-done.5 = bf16[32,32,256]{2,1,0:T(8,128)(2,1)S(1)} collective-permute-done((bf16[32,32,256]{2,1,0:T(8,128)(2,1)S(1)}, bf16[32,32,256]{2,1,0:T(8,128)(2,1)S(1)}, u32[]{:S(2)}, u32[]{:S(2)}) %collective-permute-start.5) | collective-permute-done | bytes 524320 | tf_op jit(solution)/shard_map/ppermute | solution.py:25
  184.7 2.6 fusion.1
  187.2 78.8 %all-reduce.7.cloned.1.call-done = (bf16[1,3,3,256,256]{4,3,2,1,0:T(8,128)(2,1)}, bf16[1,3,3,256,256]{4,3,2,1,0:T(8,128)(2,1)}) async-done(((bf16[1,3,3,256,256]{4,3,2,1,0:T(8,128)(2,1)}, bf16[1,3,3,256,256]{4,3,2,1,0:T(8,128)(2,1)}), (bf16[1,3,3,256,256]{4,3,2,1,0:T(8,128)(2,1)}, bf16[1,3,3,256,256]{4,3,2,1,0:T(8,128)(2,1)})) %all-reduce.7.cloned.1.call-update) | async-done | bytes 2359312 | tf_op jit(solution)/shard_map/psum | solution.py:318
  266.0 4.1 %maximum_convert_fusion = f32[2,3,3,256,256]{4,3,2,1,0:T(8,128)} fusion(bf16[1,3,3,256,256]{4,3,2,1,0:T(8,128)(2,1)} %get-tuple-element.74, bf16[1,3,3,256,256]{4,3,2,1,0:T(8,128)(2,1)} %get-tuple-element.75), kind=kLoop, calls=%fused_computation | loop fusion | flops 2359296 | bytes 7077888 | tf_op jit(solution)/shard_map/convert_element_type | solution.py:359
  (40 shorter events, 4.3 us)
Async XLA Ops:
  7.2 44.8 %collective-permute-start = (bf16[32,32,256]{2,1,0:T(8,128)(2,1)}, bf16[32,32,256]{2,1,0:T(8,128)(2,1)S(1)}, u32[]{:S(2)}, u32[]{:S(2)}) collective-permute-start(bf16[32,32,256]{2,1,0:T(8,128)(2,1)} %param.19), channel_id=1, source_target_pairs={{1,0},{2,1},{3,2},{4,3},{5,4},{6,5},{7,6},{9,8},{10,9},{11,10},{12... | collective-permute-start | bytes 1572872 | tf_op jit(solution)/shard_map/ppermute | solution.py:25
  8.5 43.5 %collective-permute-start.1 = (bf16[32,32,256]{2,1,0:T(8,128)(2,1)}, bf16[32,32,256]{2,1,0:T(8,128)(2,1)}, u32[]{:S(2)}, u32[]{:S(2)}) collective-permute-start(bf16[32,32,256]{2,1,0:T(8,128)(2,1)} %param.19), channel_id=1, source_target_pairs={{8,0},{9,1},{10,2},{11,3},{12,4},{13,5},{14,6},{15,7},{16,8},{17,9... | collective-permute-start | bytes 1572872 | tf_op jit(solution)/shard_map/ppermute | solution.py:25
  9.8 42.2 %collective-permute-start.2 = (bf16[32,32,256]{2,1,0:T(8,128)(2,1)}, bf16[32,32,256]{2,1,0:T(8,128)(2,1)}, u32[]{:S(2)}, u32[]{:S(2)}) collective-permute-start(bf16[32,32,256]{2,1,0:T(8,128)(2,1)} %param.19), channel_id=1, source_target_pairs={{9,0},{10,1},{11,2},{12,3},{13,4},{14,5},{15,6},{17,8},{18,9},{19,... | collective-permute-start | bytes 1572872 | tf_op jit(solution)/shard_map/ppermute | solution.py:25
  38.7 5.2 %copy-start.3 = (s32[16,2]{0,1:T(2,128)S(1)}, s32[16,2]{0,1:T(2,128)}, u32[]{:S(2)}) copy-start(s32[16,2]{0,1:T(2,128)} %param.22) | copy-start | bytes 388
  38.7 5.7 %copy-start.2 = (s32[16,28]{1,0:T(8,128)S(1)}, s32[16,28]{1,0:T(8,128)}, u32[]{:S(2)}) copy-start(s32[16,28]{1,0:T(8,128)} %param.23) | copy-start | bytes 5380
  38.7 57.3 %all-to-all-start = ((bf16[16,224,256]{2,1,0:T(8,128)(2,1)}), bf16[16,224,256]{2,1,0:T(8,128)(2,1)}, u32[]{:S(2)}, u32[]{:S(2)}) async-start(bf16[16,224,256]{2,1,0:T(8,128)(2,1)} %shard_map.101), calls=%async_computation | async-start | bytes 3670016 | tf_op jit(solution)/shard_map/all_to_all | solution.py:237
  43.2 222.9 %all-reduce.7.cloned.1.call-start = ((), (), s32[]{:S(2)}) async-start(), calls=%async_computation.1 | async-start | bytes 4718592 | tf_op jit(solution)/shard_map/psum | solution.py:318
  47.5 3.8 %copy-start.4 = (s32[1,8]{1,0:T(1,128)S(1)}, s32[1,8]{1,0:T(1,128)}, u32[]{:S(2)}) copy-start(s32[1,8]{1,0:T(1,128)} %param.21) | copy-start | bytes 100
  47.5 4.5 %copy-start.1 = (bf16[32,32,256]{2,1,0:T(8,128)(2,1)S(1)}, bf16[32,32,256]{2,1,0:T(8,128)(2,1)}, u32[]{:S(2)}) copy-start(bf16[32,32,256]{2,1,0:T(8,128)(2,1)} %param.19) | copy-start | bytes 1572868
  112.4 9.5 %copy-start = (f32[3,3,256,256]{3,2,1,0:T(8,128)S(1)}, f32[3,3,256,256]{3,2,1,0:T(8,128)}, u32[]{:S(2)}) copy-start(f32[3,3,256,256]{3,2,1,0:T(8,128)} %get-tuple-element.73) | copy-start | bytes 7077892
  151.0 13.0 %collective-permute-start.3 = (bf16[32,32,256]{2,1,0:T(8,128)(2,1)S(1)}, bf16[32,32,256]{2,1,0:T(8,128)(2,1)S(1)}, u32[]{:S(2)}, u32[]{:S(2)}) collective-permute-start(bf16[32,32,256]{2,1,0:T(8,128)(2,1)S(1)} %get-tuple-element.78), channel_id=1, source_target_pairs={{0,1},{1,2},{2,3},{3,4},{4,5},{5,6},{6,7},{8,9},{9,10},{10,11},{11... | collective-permute-start | bytes 1572872 | tf_op jit(solution)/shard_map/ppermute | solution.py:25
  153.3 18.5 %collective-permute-start.4 = (bf16[32,32,256]{2,1,0:T(8,128)(2,1)S(1)}, bf16[32,32,256]{2,1,0:T(8,128)(2,1)S(1)}, u32[]{:S(2)}, u32[]{:S(2)}) collective-permute-start(bf16[32,32,256]{2,1,0:T(8,128)(2,1)S(1)} %get-tuple-element.80), channel_id=1, source_target_pairs={{0,8},{1,9},{2,10},{3,11},{4,12},{5,13},{6,14},{7,15},{8,16},{9,17... | collective-permute-start | bytes 1572872 | tf_op jit(solution)/shard_map/ppermute | solution.py:25
  159.0 25.7 %collective-permute-start.5 = (bf16[32,32,256]{2,1,0:T(8,128)(2,1)S(1)}, bf16[32,32,256]{2,1,0:T(8,128)(2,1)S(1)}, u32[]{:S(2)}, u32[]{:S(2)}) collective-permute-start(bf16[32,32,256]{2,1,0:T(8,128)(2,1)S(1)} %get-tuple-element.79), channel_id=1, source_target_pairs={{0,9},{1,10},{2,11},{3,12},{4,13},{5,14},{6,15},{8,17},{9,18},{10,... | collective-permute-start | bytes 1572872 | tf_op jit(solution)/shard_map/ppermute | solution.py:25
Sparse Core Ops, SparseCore 0:
  125.5 140.4 all-reduce.6

commit v2 on v1

--- a/solution.py
+++ b/solution.py
@@ -315,7 +315,6 @@
         compiler_params=params(),
         cost_estimate=cost(2 * conv_flops, 16 * 2**20),
     )(route, incoming, slope1, slope0, x1t, back[1])
-    top_total = lax.psum(top_grads.astype(jnp.bfloat16), ("ha", "wa"))
 
     low_grads = pl.pallas_call(
         low_grads_kernel,
@@ -327,7 +326,10 @@
         compiler_params=params(),
         cost_estimate=cost(conv_flops, 8 * 2**20),
     )(pre_grad, x0t)
-    low_total = lax.psum(low_grads.astype(jnp.bfloat16), ("ha", "wa"))
+    both = jnp.stack([low_grads, top_grads]).astype(jnp.bfloat16).reshape(-1, channels)
+    share = lax.psum_scatter(both, "wa", scatter_dimension=0, tiled=True)
+    share = lax.psum(share, "ha")
+    total = lax.all_gather(share, "wa", axis=0, tiled=True)
 
     grads_ext = pl.pallas_call(
         spread_kernel,
@@ -356,7 +358,7 @@
     grad_tile = grad_tile.at[:, :BOX].add(from_left)
     grad_tile = grad_tile.at[:BOX].add(from_above)
     grad_tile = grad_tile.at[:BOX, :BOX].add(from_corner)
-    kernel_grads = jnp.stack([low_total, top_total]).astype(jnp.float32)
+    kernel_grads = total.astype(jnp.float32).reshape((LAYERS,) + grads_shape)
     return (grad_tile, kernel_grads)
 
 

time: 278 us -> 280 us (level)
  starting transfers between devices: 21.4 us -> 17.9 us
    reduce_scatter x0 -> x1, waiting for transfers between devices: none -> 46 us  [local(): share = lax.psum_scatter(both, 'wa', scatter_dimension=0, tiled=True)]
    psum x1, waiting for transfers between devices: 78.8 us -> 38 us  [local(): share = lax.psum(share, 'ha')]
    reshape x0 -> x1, other arithmetic: none -> 4.38 us  [local(): kernel_grads = total.astype(jnp.float32).reshape((LAYERS,) + grads_shape)]
    convert_element_type x1 -> x0, other arithmetic: 4.12 us -> none  [local(): kernel_grads = jnp.stack([low_total, top_total]).astype(jnp.float32)]
    ppermute x6, starting transfers between devices: 16.9 us -> 13.1 us  [shifted(): return lax.ppermute(value, ('ha', 'wa'), pairs)]
    ppermute x6, waiting for transfers between devices: 20.6 us -> 17.6 us  [shifted(): return lax.ppermute(value, ('ha', 'wa'), pairs)]
    another operation x3 -> x4, other arithmetic: 6.1 us -> 6.27 us  [the longest x2 3.59 us: local(): jnp.stack([low_grads, top_grads]).astype(jnp.bfloat16).reshape(-1, channels)]
  transfers between devices with their start and end apart: 8 -> 10, of which waited for: 3 -> 4; matrix products, arithmetic and copies ran while one was open for 10% -> 10% of each run, Pallas kernels for 25% -> 25%
where the time goes in v2:
time: 280 us; the launch traced here: 277 us
  waiting for transfers between devices  102 us (36%)
  Pallas kernels  95.8 us (34%)
  other arithmetic  21.8 us (8%)
  starting transfers between devices  17.9 us (6%)
  between operations  14.6 us (5%)
  local copies, waits for them, and re-layouts  13.8 us (5%)
  blocking collectives  11.1 us (4%)
    reduce_scatter x1, waiting for transfers between devices, local(): share = lax.psum_scatter(both, 'wa', scatter_dimension=0, tiled=True)  46 us
    psum x1, waiting for transfers between devices, local(): share = lax.psum(share, 'ha')  38 us
    pallas_call x1, Pallas kernels, local(): pl.pallas_call(forward_kernel, out_shape=(b16(channels, all_rows), b16(ch...  37.4 us
    pallas_call x1, Pallas kernels, local(): pl.pallas_call(spread_kernel, out_shape=f32(tile_rows + BOX, span, channe...  22.8 us
    ppermute x6, waiting for transfers between devices, shifted(): return lax.ppermute(value, ('ha', 'wa'), pairs)  17.6 us
    pallas_call x1, Pallas kernels, local(): pl.pallas_call(top_layer_kernel, out_shape=(f32(*grads_shape), b16(all_ro...  16.4 us
    ppermute x6, starting transfers between devices, shifted(): return lax.ppermute(value, ('ha', 'wa'), pairs)  13.1 us
    squeeze x1, blocking collectives, local(): row_counts = lax.all_gather(counts, 'wa', axis=1, tiled=True)[0]  11.1 us
  transfers between devices with their start and end apart: 10, of which 4 were waited for; matrix products, arithmetic and copies ran while one was open for 10% of the time, Pallas kernels for 25%

profile of v2, /device:TPU:0, one launch (start us, length us, event | category | flops | bytes accessed | tf_op | source)
XLA Modules:
  0.0 276.8 jit_solution(914361814458109185)
XLA Ops:
  7.2 1.3 collective-permute-start
  8.5 1.3 collective-permute-start.1
  9.8 1.3 collective-permute-start.2
  11.7 1.2 dynamic-slice.15
  13.6 11.1 %all-reduce.3 = s32[8]{0:T(128)S(1)} all-reduce(s32[8]{0:T(128)S(1)} %bitcast_dynamic-update-slice_fusion), channel_id=1, replica_groups=mesh['ha'=4,'wa'=8] {'wa'}, use_global_device_ids=true, to_apply=%add.3 | all-reduce | flops 8 | bytes 64 | tf_op jit(solution)/shard_map/squeeze | solution.py:203
  24.9 1.3 copy.15
  26.3 1.3 fusion.7
  27.6 1.2 fusion.11.index
  29.8 9.7 %shard_map.101 = bf16[16,224,256]{2,1,0:T(8,128)(2,1)} custom-call(s32[16]{0:T(128)} %fusion.11.index, bf16[8,224,256]{2,1,0:T(8,128)(2,1)} %bitcast.39), custom_call_target="tpu_custom_call" | custom-call | tf_op jit(solution)/shard_map/pallas_call | solution.py:227
  39.5 4.4 %all-to-all-start = ((bf16[16,224,256]{2,1,0:T(8,128)(2,1)}), bf16[16,224,256]{2,1,0:T(8,128)(2,1)}, u32[]{:S(2)}, u32[]{:S(2)}) async-start(bf16[16,224,256]{2,1,0:T(8,128)(2,1)} %shard_map.101), calls=%async_computation | async-start | bytes 3670016 | tf_op jit(solution)/shard_map/all_to_all | solution.py:237
  46.3 1.8 fusion.12
  48.1 1.6 copy.13
  50.3 2.9 %maximum_maximum_fusion.ext_ref = bf16[64,64,256]{2,1,0:T(8,128)(2,1)} fusion(bf16[32,32,256]{2,1,0:T(8,128)(2,1)} %collective-permute-done.2, bf16[32,32,256]{2,1,0:T(8,128)(2,1)} %collective-permute-done.1, bf16[32,32,256]{2,1,0:T(8,128)(2,1)} %collective-permute-done, bf16[32,32,256]{2,1,0:T(8,128)(2,1)S(1)} %copy-done.1), kind=kLoop, calls=%fused_computation.1 | loop fusion | flops 8388608 | bytes 4194304 | tf_op jit(solution)/shard_map/concatenate | solution.py:250
  53.2 2.0 broadcast_in_dim.66.row_ref
  55.2 1.9 broadcast_in_dim.69.col_ref
  57.2 37.4 %shard_map.102 = (bf16[256,4096]{1,0:T(8,128)(2,1)}, bf16[256,4096]{1,0:T(8,128)(2,1)}, f32[4096,256]{1,0:T(8,128)}, f32[4096,256]{1,0:T(8,128)}) custom-call(s32[16]{0:T(128)} %get-tuple-element.82.tops, bf16[64,64,256]{2,1,0:T(8,128)(2,1)} %maximum_maximum_fusion.ext_ref, f32[4096,128]{1,0:T(8,128)} %broadcast_in_dim.66.row_ref, ...), custom_call_target="tpu_custom_call" | custom-call | flops 13958643712 | bytes 25165824 | tf_op jit(solution)/shard_map/pallas_call | solution.py:276
  94.6 16.4 %shard_map.103 = (f32[3,3,256,256]{3,2,1,0:T(8,128)}, bf16[4096,256]{1,0:T(8,128)(2,1)}) custom-call(s32[2,16]{1,0:T(2,128)} %pad_add_fusion.route, bf16[16,224,256]{2,1,0:T(8,128)(2,1)} %all-to-all-done.inc_ref, f32[4096,256]{1,0:T(8,128)} %get-tuple-element.68.s1_ref, f32[4096,256]{1,0:T(8,128)} %get-tuple-element.69.s0_ref, ...), custom_call_target="tpu_custom_call" | custom-call | flops 9663676416 | bytes 16777216 | tf_op jit(solution)/shard_map/pallas_call | solution.py:299
  111.0 9.5 %shard_map.105 = f32[3,3,256,256]{3,2,1,0:T(8,128)} custom-call(bf16[4096,256]{1,0:T(8,128)(2,1)} %get-tuple-element.71.pg_ref, bf16[256,4096]{1,0:T(8,128)(2,1)} %get-tuple-element.72.x0t_ref), custom_call_target="tpu_custom_call" | custom-call | flops 4831838208 | bytes 8388608 | tf_op jit(solution)/shard_map/pallas_call | solution.py:319
  120.5 2.0 convert_bitcast_fusion
  122.5 1.6 pad_maximum_fusion
  124.2 46.0 %reduce-scatter.2.cloned.1.call-done = bf16[576,256]{1,0:T(8,128)(2,1)} async-done(((bf16[4608,256]{1,0:T(8,128)(2,1)}), bf16[576,256]{1,0:T(8,128)(2,1)}) %reduce-scatter.2.cloned.1.call-update) | async-done | bytes 294928 | tf_op jit(solution)/shard_map/reduce_scatter | solution.py:330
  170.5 38.0 %all-reduce.6.cloned.1.call-done = bf16[576,256]{1,0:T(8,128)(2,1)} async-done(((bf16[576,256]{1,0:T(8,128)(2,1)}), bf16[576,256]{1,0:T(8,128)(2,1)}) %all-reduce.6.cloned.1.call-update) | async-done | bytes 294928 | tf_op jit(solution)/shard_map/psum | solution.py:331
  208.7 1.5 copy.14
  210.9 22.8 %shard_map.104 = f32[64,64,256]{2,1,0:T(8,128)} custom-call(s32[16]{0:T(128)} %get-tuple-element.82.tops, bf16[4096,256]{1,0:T(8,128)(2,1)} %get-tuple-element.71.pg_ref, f32[16,2,256]{2,1,0:T(2,128)} %pad_maximum_fusion.1.place_ref, bf16[3,768,256]{2,1,0:T(8,128)(2,1)} %bitcast.44), custom_call_target="tpu_custom_call" | custom-call | flops 9126805504 | bytes 8388608 | tf_op jit(solution)/shard_map/pallas_call | solution.py:334
  233.7 2.5 convert.14
  236.4 1.3 collective-permute-start.3
  237.7 3.3 %collective-permute-start.4 = (bf16[32,32,256]{2,1,0:T(8,128)(2,1)S(1)}, bf16[32,32,256]{2,1,0:T(8,128)(2,1)S(1)}, u32[]{:S(2)}, u32[]{:S(2)}) collective-permute-start(bf16[32,32,256]{2,1,0:T(8,128)(2,1)S(1)} %get-tuple-element.78), channel_id=1, source_target_pairs={{0,8},{1,9},{2,10},{3,11},{4,12},{5,13},{6,14},{7,15},{8,16},{9,17... | collective-permute-start | bytes 1572872 | tf_op jit(solution)/shard_map/ppermute | solution.py:25
  241.0 4.6 %collective-permute-start.5 = (bf16[32,32,256]{2,1,0:T(8,128)(2,1)S(1)}, bf16[32,32,256]{2,1,0:T(8,128)(2,1)S(1)}, u32[]{:S(2)}, u32[]{:S(2)}) collective-permute-start(bf16[32,32,256]{2,1,0:T(8,128)(2,1)S(1)} %get-tuple-element.77), channel_id=1, source_target_pairs={{0,9},{1,10},{2,11},{3,12},{4,13},{5,14},{6,15},{8,17},{9,18},{10,... | collective-permute-start | bytes 1572872 | tf_op jit(solution)/shard_map/ppermute | solution.py:25
  245.7 6.4 %collective-permute-done.4 = bf16[32,32,256]{2,1,0:T(8,128)(2,1)S(1)} collective-permute-done((bf16[32,32,256]{2,1,0:T(8,128)(2,1)S(1)}, bf16[32,32,256]{2,1,0:T(8,128)(2,1)S(1)}, u32[]{:S(2)}, u32[]{:S(2)}) %collective-permute-start.4) | collective-permute-done | bytes 524320 | tf_op jit(solution)/shard_map/ppermute | solution.py:25
  252.1 11.2 %collective-permute-done.5 = bf16[32,32,256]{2,1,0:T(8,128)(2,1)S(1)} collective-permute-done((bf16[32,32,256]{2,1,0:T(8,128)(2,1)S(1)}, bf16[32,32,256]{2,1,0:T(8,128)(2,1)S(1)}, u32[]{:S(2)}, u32[]{:S(2)}) %collective-permute-start.5) | collective-permute-done | bytes 524320 | tf_op jit(solution)/shard_map/ppermute | solution.py:25
  263.3 2.6 fusion.1
  265.9 4.4 %convert.17 = f32[2,3,3,256,256]{4,3,2,1,0:T(8,128)} convert(bf16[2,3,3,256,256]{4,3,2,1,0:T(8,128)(2,1)} %bitcast.40) | non-fusion elementwise | flops 1179648 | bytes 7077888 | tf_op jit(solution)/shard_map/reshape | solution.py:361
  (47 shorter events, 6.2 us)
Async XLA Ops:
  7.2 43.2 %collective-permute-start = (bf16[32,32,256]{2,1,0:T(8,128)(2,1)}, bf16[32,32,256]{2,1,0:T(8,128)(2,1)}, u32[]{:S(2)}, u32[]{:S(2)}) collective-permute-start(bf16[32,32,256]{2,1,0:T(8,128)(2,1)} %param.19), channel_id=1, source_target_pairs={{1,0},{2,1},{3,2},{4,3},{5,4},{6,5},{7,6},{9,8},{10,9},{11,10},{12... | collective-permute-start | bytes 1572872 | tf_op jit(solution)/shard_map/ppermute | solution.py:25
  8.5 41.9 %collective-permute-start.1 = (bf16[32,32,256]{2,1,0:T(8,128)(2,1)}, bf16[32,32,256]{2,1,0:T(8,128)(2,1)}, u32[]{:S(2)}, u32[]{:S(2)}) collective-permute-start(bf16[32,32,256]{2,1,0:T(8,128)(2,1)} %param.19), channel_id=1, source_target_pairs={{8,0},{9,1},{10,2},{11,3},{12,4},{13,5},{14,6},{15,7},{16,8},{17,9... | collective-permute-start | bytes 1572872 | tf_op jit(solution)/shard_map/ppermute | solution.py:25
  9.8 40.6 %collective-permute-start.2 = (bf16[32,32,256]{2,1,0:T(8,128)(2,1)}, bf16[32,32,256]{2,1,0:T(8,128)(2,1)}, u32[]{:S(2)}, u32[]{:S(2)}) collective-permute-start(bf16[32,32,256]{2,1,0:T(8,128)(2,1)} %param.19), channel_id=1, source_target_pairs={{9,0},{10,1},{11,2},{12,3},{13,4},{14,5},{15,6},{17,8},{18,9},{19,... | collective-permute-start | bytes 1572872 | tf_op jit(solution)/shard_map/ppermute | solution.py:25
  39.5 5.8 %copy-start.3 = (s32[16,2]{0,1:T(2,128)S(1)}, s32[16,2]{0,1:T(2,128)}, u32[]{:S(2)}) copy-start(s32[16,2]{0,1:T(2,128)} %param.22) | copy-start | bytes 388
  39.5 6.3 %copy-start.2 = (s32[16,28]{1,0:T(8,128)S(1)}, s32[16,28]{1,0:T(8,128)}, u32[]{:S(2)}) copy-start(s32[16,28]{1,0:T(8,128)} %param.23) | copy-start | bytes 5380
  39.5 55.1 %all-to-all-start = ((bf16[16,224,256]{2,1,0:T(8,128)(2,1)}), bf16[16,224,256]{2,1,0:T(8,128)(2,1)}, u32[]{:S(2)}, u32[]{:S(2)}) async-start(bf16[16,224,256]{2,1,0:T(8,128)(2,1)} %shard_map.101), calls=%async_computation | async-start | bytes 3670016 | tf_op jit(solution)/shard_map/all_to_all | solution.py:237
  44.0 126.3 %reduce-scatter.2.cloned.1.call-start = ((), (), s32[]{:S(2)}) async-start(), calls=%async_computation.2 | async-start | bytes 2654208 | tf_op jit(solution)/shard_map/reduce_scatter | solution.py:330
  48.0 1.6 copy-start.4
  48.0 2.3 copy-start.1
  111.0 9.5 %copy-start = (f32[3,3,256,256]{3,2,1,0:T(8,128)S(1)}, f32[3,3,256,256]{3,2,1,0:T(8,128)}, u32[]{:S(2)}) copy-start(f32[3,3,256,256]{3,2,1,0:T(8,128)} %get-tuple-element.73) | copy-start | bytes 7077892
  124.2 84.3 %all-reduce.6.cloned.1.call-start = ((), (), s32[]{:S(2)}) async-start(), calls=%async_computation.3 | async-start | bytes 589824 | tf_op jit(solution)/shard_map/psum | solution.py:331
  170.2 95.6 %all-gather.2.cloned.1.call-start = ((), (), s32[]{:S(2)}) async-start(), calls=%async_computation.4 | async-start | bytes 2654208 | tf_op jit(solution)/shard_map/all_gather | solution.py:332
  236.4 9.3 %collective-permute-start.3 = (bf16[32,32,256]{2,1,0:T(8,128)(2,1)S(1)}, bf16[32,32,256]{2,1,0:T(8,128)(2,1)S(1)}, u32[]{:S(2)}, u32[]{:S(2)}) collective-permute-start(bf16[32,32,256]{2,1,0:T(8,128)(2,1)S(1)} %get-tuple-element.76), channel_id=1, source_target_pairs={{0,1},{1,2},{2,3},{3,4},{4,5},{5,6},{6,7},{8,9},{9,10},{10,11},{11... | collective-permute-start | bytes 1572872 | tf_op jit(solution)/shard_map/ppermute | solution.py:25
  237.7 14.4 %collective-permute-start.4 = (bf16[32,32,256]{2,1,0:T(8,128)(2,1)S(1)}, bf16[32,32,256]{2,1,0:T(8,128)(2,1)S(1)}, u32[]{:S(2)}, u32[]{:S(2)}) collective-permute-start(bf16[32,32,256]{2,1,0:T(8,128)(2,1)S(1)} %get-tuple-element.78), channel_id=1, source_target_pairs={{0,8},{1,9},{2,10},{3,11},{4,12},{5,13},{6,14},{7,15},{8,16},{9,17... | collective-permute-start | bytes 1572872 | tf_op jit(solution)/shard_map/ppermute | solution.py:25
  241.0 22.3 %collective-permute-start.5 = (bf16[32,32,256]{2,1,0:T(8,128)(2,1)S(1)}, bf16[32,32,256]{2,1,0:T(8,128)(2,1)S(1)}, u32[]{:S(2)}, u32[]{:S(2)}) collective-permute-start(bf16[32,32,256]{2,1,0:T(8,128)(2,1)S(1)} %get-tuple-element.77), channel_id=1, source_target_pairs={{0,9},{1,10},{2,11},{3,12},{4,13},{5,14},{6,15},{8,17},{9,18},{10,... | collective-permute-start | bytes 1572872 | tf_op jit(solution)/shard_map/ppermute | solution.py:25
Sparse Core Ops, SparseCore 0:
  124.3 45.8 reduce-scatter.1
  172.7 35.7 all-reduce.5
  210.5 29.0 all-gather.1
